TPU v7x, 512 devices: a whole 4x4x16 slice. The times are simulated.
512 devices in a mesh: row: 32 (over y, z_lo), col: 16 (over x, z_hi, core).
Axes of the slice: x: 4, y: 4, z: 16 (z_hi: 2, z_lo: 8; z = z_hi * 8 + z_lo), core: 2. Of those that a mesh axis runs over, the one named last changes fastest.
Arguments:
- cotangent: bfloat16 [16, 256, 256], P('col', 'row'), may hold values from -0.125 to 0.125
- preact_two: bfloat16 [16, 256, 256], P('col', 'row'), may hold values from -6 to 6
- aggregate_two: bfloat16 [16, 256, 256], P('col', 'row'), may hold values from 0 to 2
- self_hidden: bfloat16 [16, 256, 256], P('col', 'row'), may hold values from 0 to 2
- neigh_weight: bfloat16 [256, 256], replicated, may hold values from -0.375 to 0.375
- root_weight: bfloat16 [256, 256], replicated, may hold values from -0.375 to 0.375
- sampled_tiles: bfloat16 [32, 16, 16, 128, 128], P('row', 'col'), may hold values from 0 to 0.049804688
- tile_slot: int32 [32, 16, 16], P('row', 'col'), may hold values from 0 to 31, as said below
- tile_count: int32 [32, 16], P('row', 'col'), may hold values from 1 to 16, as said below
- target_self: int32 [16, 256], P('col'), may hold values from 0 to 65535, as said below
- preact_one: bfloat16 [32, 2048, 256], P('row', 'col'), may hold values from -6 to 6
- aggregate_one: bfloat16 [32, 2048, 768], P('row', 'col'), may hold values from -6 to 6
- feature_one: bfloat16 [32, 2048, 768], P('row', 'col'), may hold values from -6 to 6
Outputs:
- layer_two_grads: float32 [2, 256, 256], replicated
- layer_one_grads: float32 [2, 768, 256], replicated
Inputs may be any that keep to these rules, and one draw needn't show every extreme that they name: `tile_slot`: within one block the 16 slots hold distinct positions; position s is tile row s // 16 and tile column s % 16 of the block. `tile_count`: slots from a block's count on hold no tile. Some block is full in every draw. `target_self`: all values are distinct.
All inputs are finite; a program needn't handle non-finite values.
Results may differ from a plain program's by a relative error of at most 0.013.
Values may be sent and summed in bfloat16 or wider, within the bound.
No kernel may reach another device: no remote copies, remote signals or barrier semaphores. Data moves between devices by JAX's collectives and lax.ppermute only.
A program may use at most 64 MiB of HBM per device.

v0:
```python
import math

import jax
import jax.numpy as jnp
from jax import lax
from jax.sharding import PartitionSpec as P


def project(delta_rows, weight_matrix):
    contract_last = (((1,), (1,)), ((), ()))
    return lax.dot_general(
        delta_rows, weight_matrix, contract_last, preferred_element_type=jnp.float32
    ).astype(jnp.bfloat16)


def stacked_terms(left_first, left_second, delta_rows):
    contract_first = (((0,), (0,)), ((), ()))
    first_term = lax.dot_general(
        left_first, delta_rows, contract_first, preferred_element_type=jnp.float32
    )
    second_term = lax.dot_general(
        left_second, delta_rows, contract_first, preferred_element_type=jnp.float32
    )
    return jnp.stack([first_term, second_term])


def local(
    cotangent,
    preact_two,
    aggregate_two,
    self_hidden,
    neigh_weight,
    root_weight,
    sampled_tiles,
    tile_slot,
    tile_count,
    target_self,
    preact_one,
    aggregate_one,
    feature_one,
):
    delta_two = jnp.where(preact_two[0] > 0, cotangent[0], jnp.zeros_like(cotangent[0]))
    two_terms = stacked_terms(aggregate_two[0], self_hidden[0], delta_two)
    gathered = lax.all_gather(delta_two, "row", axis=0, tiled=True)
    message = project(gathered, neigh_weight)
    selfward = project(gathered, root_weight)
    tile_edge = sampled_tiles.shape[-1]
    capacity = sampled_tiles.shape[2]
    hidden_width = message.shape[1]
    source_rows = preact_one.shape[1] * lax.axis_size("col")
    source_tiles = source_rows // tile_edge
    message_tiles = message.reshape(message.shape[0] // tile_edge, tile_edge, hidden_width)
    group_size = math.gcd(capacity, 16)
    filled = tile_count[0, 0]
    group_turns = (filled + group_size - 1) // group_size
    tile_block = sampled_tiles[0, 0]
    slot_block = tile_slot[0, 0]

    def tile_step(turn, partial_value):
        first_slot = turn * group_size
        alive_mask = first_slot + jnp.arange(group_size, dtype=jnp.int32) < filled
        picked = jnp.take(message_tiles, slot_block // source_tiles, axis=0)
        contrib = jnp.einsum("kij,kif->kjf", tile_block, picked, preferred_element_type=jnp.float32)
        contrib = jnp.where(alive_mask[:, None, None], contrib, jnp.zeros_like(contrib))
        return partial_value.at[slot_block % source_tiles].add(contrib)

    partial_value = lax.fori_loop(
        0, group_turns, tile_step, jnp.zeros((source_tiles, tile_edge, hidden_width), jnp.float32)
    )
    partial_value = partial_value.reshape(source_rows, hidden_width)
    local_row = target_self[0] - lax.axis_index("row") * source_rows
    target_row = jnp.where((local_row >= 0) & (local_row < source_rows), local_row, source_rows)
    partial_value = partial_value.at[target_row].add(selfward.astype(jnp.float32), mode="drop")
    summed = lax.psum_scatter(
        partial_value.astype(jnp.bfloat16), "col", scatter_dimension=0, tiled=True
    ).astype(jnp.float32)
    delta_one = jnp.where(preact_one[0] > 0, summed, jnp.zeros_like(summed)).astype(jnp.bfloat16)
    one_terms = stacked_terms(aggregate_one[0], feature_one[0], delta_one)
    layer_two, layer_one = lax.psum((two_terms, one_terms), ("row", "col"))
    return (layer_two, layer_one)


def solution(mesh):
    in_specs = (
        P("col", "row", None),
        P("col", "row", None),
        P("col", "row", None),
        P("col", "row", None),
        P(),
        P(),
        P("row", "col", None, None, None),
        P("row", "col", None),
        P("row", "col"),
        P("col", None),
        P("row", "col", None),
        P("row", "col", None),
        P("row", "col", None),
    )
    out_specs = (P(), P())
    return jax.shard_map(local, mesh=mesh, in_specs=in_specs, out_specs=out_specs, check_vma=False)
```

profile of v0, /device:TPU:1, one launch (start us, length us, event | category | flops | bytes accessed | tf_op | source)
XLA Modules:
  0.0 743.7 jit_solution(8222287208336013115)
XLA Ops:
  7.2 0.0 copy-start
  7.2 0.0 copy-start.6
  7.2 0.0 copy-start.1
  7.2 0.0 reduce-scatter.2.cloned.1.call-start
  8.0 0.7 sign_bitcast_fusion
  8.6 0.7 bitcast_negate_fusion
  9.3 0.7 compare_select_fusion.9
  10.0 113.0 %all-gather = bf16[1,256,256]{2,1,0:T(8,128)(2,1)S(1)} all-gather(bf16[1,8,256]{2,1,0:T(8,128)(2,1)S(1)} %compare_select_fusion.9), channel_id=2, replica_groups=mesh['row'=32,'col'=16] {'row'}, dimensions={1}, use_global_device_ids=true | all-gather | bytes 135168 | tf_op jit(solution)/shard_map/all_gather | solution.py:44
  123.0 1.1 convolution_convert_fusion.1
  124.2 1.6 broadcast.364
  125.7 9.6 %while.14 = (s32[]{:T(128)}, f32[16,128,256]{2,1,0:T(8,128)}, s32[]{:T(128)}, s32[16]{0:T(128)S(1)}, s32[16,1]{0,1:T(1,128)S(1)}, /*index=5*/s32[]{:T(128)}, s32...) while((s32[]{:T(128)}, f32[16,128,256]{2,1,0:T(8,128)}, ...), condition=%wide.region_3.4_spmd, body=%wide.region_1.3_spmd.sunk | while | flops 135792320 | bytes 16257937 | solution.py:67
  125.8 0.7 compare_and_fusion.2
  126.5 0.6 gather_fusion
  127.1 1.9 select_bitcast_fusion.2
  129.0 1.9 copy.25
  130.9 4.4 scatter_fusion
  135.4 0.2 fusion.6
  135.6 4.7 scatter_fusion.1
  140.3 2.7 convert_element_type.21
  143.0 0.0 reduce-scatter.2.cloned.1.call-update
  143.0 0.0 all-reduce.3.cloned.1.call-start
  143.1 0.2 convolution_bitcast_fusion.2
  143.3 0.2 convolution_bitcast_fusion.3
  143.5 0.8 pad_maximum_fusion.1
  144.4 112.9 %reduce-scatter.2.cloned.1.call-done = bf16[128,256]{1,0:T(8,128)(2,1)} async-done(((bf16[2048,256]{1,0:T(8,128)(2,1)}), bf16[128,256]{1,0:T(8,128)(2,1)}) %reduce-scatter.2.cloned.1.call-update) | async-done | bytes 65552 | tf_op jit(solution)/shard_map/reduce_scatter | solution.py:74
  257.3 1.1 convolution_bitcast_fusion
  258.4 1.1 convolution_bitcast_fusion.1
  259.5 1.2 pad_maximum_fusion
  260.8 0.0 all-reduce.3.cloned.1.call-update
  260.8 472.0 %all-reduce.3.cloned.1.call-done = (f32[2,256,256]{1,2,0:T(8,128)}, f32[2,768,256]{1,2,0:T(8,128)}) async-done(((f32[2,256,256]{1,2,0:T(8,128)}, f32[2,768,256]{1,2,0:T(8,128)}), (f32[2,256,256]{1,2,0:T(8,128)}, f32[2,768,256]{1,2,0:T(8,128)})) %all-reduce.3.cloned.1.call-update) | async-done | bytes 2097168 | tf_op jit(solution)/shard_map/psum | solution.py:79
  732.8 3.1 copy.22
  735.8 1.0 copy.21
  (20 shorter events, 0.1 us)
Async XLA Ops:
  7.2 250.1 %copy-start = (bf16[1,128,768]{2,1,0:T(8,128)(2,1)S(1)}, bf16[1,128,768]{2,1,0:T(8,128)(2,1)}, u32[]{:S(2)}) copy-start(bf16[1,128,768]{2,1,0:T(8,128)(2,1)} %param.27) | copy-start | bytes 589828
  7.2 118.5 %copy-start.6 = (s32[1,1,16]{2,1,0:T(1,128)S(1)}, s32[1,1,16]{2,1,0:T(1,128)}, u32[]{:S(2)}) copy-start(s32[1,1,16]{2,1,0:T(1,128)} %param.22) | copy-start | bytes 196
  7.2 118.5 %copy-start.1 = (bf16[1,1,16,128,128]{4,3,2,1,0:T(8,128)(2,1)S(1)}, bf16[1,1,16,128,128]{4,3,2,1,0:T(8,128)(2,1)}, u32[]{:S(2)}) copy-start(bf16[1,1,16,128,128]{4,3,2,1,0:T(8,128)(2,1)} %param.21) | copy-start | bytes 1572868
  7.2 250.0 %reduce-scatter.2.cloned.1.call-start = ((), (), s32[]{:S(2)}) async-start(), calls=%async_computation.1 | async-start | bytes 1114112 | tf_op jit(solution)/shard_map/reduce_scatter | solution.py:74
  125.7 9.6 %copy-start.5 = (bf16[256,256]{1,0:T(8,128)(2,1)S(1)}, bf16[256,256]{1,0:T(8,128)(2,1)}, u32[]{:S(2)}) copy-start(bf16[256,256]{1,0:T(8,128)(2,1)} %param.20) | copy-start | bytes 393220
  125.7 9.9 %copy-start.9 = (s32[1,256]{1,0:T(1,128)S(1)}, s32[1,256]{1,0:T(1,128)}, u32[]{:S(2)}) copy-start(s32[1,256]{1,0:T(1,128)} %param.24) | copy-start | bytes 3076
  140.3 2.8 copy-start.7
  140.3 3.0 copy-start.8
  143.0 114.3 %copy-start.3 = (bf16[1,128,256]{2,1,0:T(8,128)(2,1)S(1)}, bf16[1,128,256]{2,1,0:T(8,128)(2,1)}, u32[]{:S(2)}) copy-start(bf16[1,128,256]{2,1,0:T(8,128)(2,1)} %param.25) | copy-start | bytes 196612
  143.0 115.4 %copy-start.4 = (bf16[1,128,768]{2,1,0:T(8,128)(2,1)S(1)}, bf16[1,128,768]{2,1,0:T(8,128)(2,1)}, u32[]{:S(2)}) copy-start(bf16[1,128,768]{2,1,0:T(8,128)(2,1)} %param.26) | copy-start | bytes 589828
  143.0 589.7 %all-reduce.3.cloned.1.call-start = ((), (), s32[]{:S(2)}) async-start(), calls=%async_computation.2 | async-start | bytes 4194304 | tf_op jit(solution)/shard_map/psum | solution.py:79
  732.8 3.1 copy-start.2
Sparse Core Ops, SparseCore 0:
  143.1 114.0 reduce-scatter.1
  264.1 468.5 all-reduce.2
where the time goes:
time: 744 us
  waiting for transfers between devices  585 us (79%)
  blocking collectives  113 us (15%)
  other arithmetic  16.6 us (2%)
  between operations  14.9 us (2%)
  local copies, waits for them, and re-layouts  8.2 us (1%)
    psum x1, waiting for transfers between devices, local(): layer_two, layer_one = lax.psum((two_terms, one_terms), ('row', 'col'))  472 us
    all_gather x1, blocking collectives, local(): gathered = lax.all_gather(delta_two, 'row', axis=0, tiled=True)  113 us
    reduce_scatter x1, waiting for transfers between devices, local(): lax.psum_scatter(partial_value.astype(jnp.bfloat16), 'col', scatter_dimen...  113 us
  transfers between devices with their start and end apart: 2, of which 2 were waited for; matrix products, arithmetic and copies ran while one was open for 0% of the time, Pallas kernels for 0%

commit v1 on v0

v1 whole, which is shorter than its diff:
```python
import jax
import jax.numpy as jnp
from jax import lax
from jax.experimental import pallas as pl
from jax.experimental.pallas import tpu as pltpu
from jax.sharding import PartitionSpec as P

ROW = ("y", "zm", "zna", "znb")
COL = ("x", "zh", "core")
PAIRED_PLANE = ("znb", "y", "x")
VMEM = pl.BlockSpec(memory_space=pltpu.VMEM)
SMEM = pl.BlockSpec(memory_space=pltpu.SMEM)
HBM = pl.BlockSpec(memory_space=pltpu.HBM)
ANY = pl.BlockSpec(memory_space=pl.ANY)
ROWS_BOTH = (((0,), (0,)), ((), ()))
LAST_BOTH = (((1,), (1,)), ((), ()))


def exchange(blocks, axes):
    return lax.all_to_all(blocks, axes, 0, 0, tiled=True)


def spread(block, axes, n):
    return exchange(jnp.broadcast_to(block[None], (n,) + block.shape), axes)


def swap(value, axis):
    return lax.ppermute(value, axis, [(0, 1), (1, 0)])


def dot(left, right, dims=(((1,), (0,)), ((), ()))):
    return lax.dot_general(left, right, dims, preferred_element_type=jnp.float32)


def fetch(pairs, sems):
    copies = [pltpu.make_async_copy(source, target, sems.at[at]) for at, (source, target) in enumerate(pairs)]
    for copy in copies:
        copy.start()
    return copies


def mask_kernel(cot_ref, preact_ref, copies_ref, held, sems):
    for copy in fetch([(cot_ref, held.at[0]), (preact_ref, held.at[1])], sems):
        copy.wait()
    delta = masked(held[0], held[1])
    for at in range(copies_ref.shape[0]):
        copies_ref[at] = delta


def masked(value, preact):
    return jnp.where(preact.astype(jnp.float32) > 0, value.astype(jnp.float32), 0.0).astype(jnp.bfloat16)


def layout_kernel(slot_ref, count_ref, tiles_ref, target_ref, neigh_ref, root_ref, layout_ref, weight_ref):
    base = lax.axis_index(ROW) * 2048
    target = target_ref[...] - base
    layout_ref[:, :, :256] = jnp.zeros((16, 128, 256), jnp.bfloat16)
    for at in range(16):
        rows = lax.broadcasted_iota(jnp.int32, (128, 256), 0) + at * 128
        layout_ref[at, :, 256:] = jnp.where(rows == target, 1.0, 0.0).astype(jnp.bfloat16)
    weight_ref[0] = neigh_ref[...]
    weight_ref[1] = root_ref[...]
    count = count_ref[0, 0]
    for k in range(16):
        slot = slot_ref[0, k]
        for t in range(2):

            @pl.when((k < count) & (slot // 16 == t))
            def _():
                layout_ref[slot % 16, :, t * 128 : (t + 1) * 128] = tiles_ref[k].T


def bundle_kernel(agg_one_ref, feat_one_ref, preact_ref, cot_ref, pre_two_ref, agg_two_ref, self_ref, bundle_ref):
    bundle_ref[:128, :768] = agg_one_ref[...]
    bundle_ref[:128, 768:1536] = feat_one_ref[...]
    bundle_ref[:128, 1536:] = preact_ref[...]
    for at, ref in enumerate((cot_ref, pre_two_ref, agg_two_ref, self_ref)):
        padded = jnp.concatenate([ref[...].astype(jnp.float32), jnp.zeros((8, 256), jnp.float32)])
        bundle_ref[128:, at * 256 : (at + 1) * 256] = padded.astype(jnp.bfloat16)
    bundle_ref[128:, 1024:] = jnp.zeros((16, 768), jnp.bfloat16)


def by_core(body):
    core = lax.axis_index("core")
    for at in range(2):
        pl.when(core == at)(lambda at=at: body(at, slice(at * 128, at * 128 + 128), slice(128 - at * 128, 256 - at * 128)))


def turn_kernel(own_ref, recv_ref, turned_ref, preact_ref, two_ref):
    def body(core, mine, other):
        preact = slice(1536 + core * 128, 1664 + core * 128)
        two = [0.0, 0.0]
        for ref, rows in ((own_ref, mine), (recv_ref, other)):
            turned_ref[:, rows] = ref[:128, :1536].T
            preact_ref[rows] = ref[:128, preact]
            delta = masked(ref[128:, mine], ref[128:, 256 + core * 128 : 384 + core * 128])
            two[0] += dot(ref[128:, 512:768], delta, ROWS_BOTH)
            two[1] += dot(ref[128:, 768:1024], delta, ROWS_BOTH)
        two_ref[:256] = two[0].astype(jnp.bfloat16)
        two_ref[256:] = two[1].astype(jnp.bfloat16)

    by_core(body)


def product(delta_ref, weight_ref, layout_ref, columns):
    delta = delta_ref[...]
    message = [dot(delta, weight_ref[at, columns], LAST_BOTH).astype(jnp.bfloat16) for at in range(2)]
    return dot(layout_ref[...], jnp.concatenate(message))


def send_kernel(delta_ref, weight_ref, layout_ref, send_ref):
    def body(core, mine, other):
        send_ref[...] = product(delta_ref, weight_ref, layout_ref, other).astype(jnp.bfloat16)

    by_core(body)


def keep_kernel(delta_ref, weight_ref, layout_ref, keep_ref):
    def body(core, mine, other):
        keep_ref[...] = product(delta_ref, weight_ref, layout_ref, mine)

    by_core(body)


def pair_kernel(keep_ref, recv_ref, sum_ref):
    sum_ref[...] = (keep_ref[...] + recv_ref[...].astype(jnp.float32)).astype(jnp.bfloat16)


def terms_kernel(keep_ref, recv_ref, preact_ref, turned_ref, two_ref, terms_ref):
    delta = masked(keep_ref[...] + recv_ref[...].astype(jnp.float32), preact_ref[...])
    terms_ref[:1536] = dot(turned_ref[...], delta).astype(jnp.bfloat16)
    terms_ref[1536:] = two_ref[...]


def widen_half(half, value_ref, two_ref, one_ref, wide, sems):
    columns = pl.ds(pl.multiple_of(half * 128, 128), 128)
    copies = []
    for turn in range(4):
        rows = pl.ds(turn * 512, 512)
        target = one_ref.at[rows, columns] if turn < 3 else two_ref.at[:, columns]
        copies.append(pltpu.make_async_copy(wide.at[rows], target, sems.at[turn]))
        wide[rows] = value_ref[rows].astype(jnp.float32)
        copies[-1].start()
    for copy in copies:
        copy.wait()


def widen_own_kernel(own_ref, two_ref, one_ref, wide, sems):
    widen_half(lax.axis_index("core"), own_ref, two_ref, one_ref, wide, sems)


def widen_recv_kernel(recv_ref, two_in, one_in, two_ref, one_ref, wide, sems):
    widen_half(1 - lax.axis_index("core"), recv_ref, two_ref, one_ref, wide, sems)


def shape(dims, kind=jnp.bfloat16):
    return jax.ShapeDtypeStruct(dims, kind)


def call(kernel, outs, ins, *operands, flops=1_000_000, moved=1_000_000, vmem=16, **rest):
    return pl.pallas_call(
        kernel,
        out_shape=outs,
        in_specs=ins,
        compiler_params=pltpu.CompilerParams(vmem_limit_bytes=vmem * 2**20),
        cost_estimate=pl.CostEstimate(flops=flops, bytes_accessed=moved, transcendentals=0),
        name=kernel.__name__.replace("_kernel", ""),
        **rest,
    )(*operands)


def local(
    cotangent,
    preact_two,
    aggregate_two,
    self_hidden,
    neigh_weight,
    root_weight,
    sampled_tiles,
    tile_slot,
    tile_count,
    target_self,
    preact_one,
    aggregate_one,
    feature_one,
):
    zh = lax.axis_index("zh")
    copies = call(
        mask_kernel,
        shape((32, 8, 256)),
        [HBM] * 2,
        cotangent[0],
        preact_two[0],
        flops=10_000,
        moved=140_000,
        vmem=60,
        out_specs=VMEM,
        scratch_shapes=[pltpu.VMEM((2, 8, 256), jnp.bfloat16), pltpu.SemaphoreType.DMA((2,))],
    )
    gathered = exchange(copies, ROW).reshape(256, 256)
    layout, weight = call(
        layout_kernel,
        (shape((16, 128, 512)), shape((2, 256, 256))),
        [SMEM] * 2 + [VMEM] * 4,
        tile_slot[0],
        tile_count,
        sampled_tiles[0, 0],
        target_self,
        neigh_weight,
        root_weight,
        moved=3_000_000,
        out_specs=(VMEM, VMEM),
    )
    layout = layout.reshape(2048, 512)
    send = call(send_kernel, shape((2048, 128)), [VMEM] * 3, gathered, weight, layout, flops=300_000_000, out_specs=VMEM)
    recv = swap(send, "core")
    keep = call(
        keep_kernel,
        shape((2048, 128), jnp.float32),
        [VMEM] * 3,
        gathered,
        weight,
        layout,
        flops=300_000_000,
        moved=3_000_000,
        out_specs=VMEM,
    )
    blocks = call(pair_kernel, shape((2048, 128)), [VMEM] * 2, keep, recv, out_specs=VMEM)
    late = (aggregate_one, feature_one, preact_one, cotangent, preact_two, aggregate_two, self_hidden)
    blocks, late = lax.optimization_barrier((blocks, late))
    bundle = call(
        bundle_kernel,
        shape((144, 1792)),
        [VMEM] * 7,
        *(value[0] for value in late),
        out_specs=VMEM,
    )
    turned, preact, two_terms = call(
        turn_kernel,
        (shape((1536, 256)), shape((256, 128)), shape((512, 128))),
        [VMEM] * 2,
        bundle,
        swap(bundle, "core"),
        moved=2_000_000,
        out_specs=(VMEM,) * 3,
    )
    blocks = exchange(blocks.reshape(4, 2, 256, 128), ("x",)).astype(jnp.float32).sum(0)
    keep = lax.dynamic_index_in_dim(blocks, zh, 0, keepdims=False)
    send = lax.dynamic_index_in_dim(blocks, 1 - zh, 0, keepdims=False).astype(jnp.bfloat16)
    terms = call(
        terms_kernel,
        shape((2048, 128)),
        [VMEM] * 5,
        keep,
        swap(send, "zh"),
        preact,
        turned,
        two_terms,
        flops=100_000_000,
        out_specs=VMEM,
    )
    terms = exchange(terms.reshape(32, 64, 128), PAIRED_PLANE).astype(jnp.float32).sum(0)
    terms = spread(terms.astype(jnp.bfloat16), ("zna", "zm", "zh"), 8).astype(jnp.float32).sum(0)
    terms = spread(terms.astype(jnp.bfloat16), PAIRED_PLANE, 32).reshape(2048, 128)
    recv = swap(terms, "core")
    outs = (shape((512, 256), jnp.float32), shape((1536, 256), jnp.float32))
    scratch = [pltpu.VMEM((2048, 128), jnp.float32), pltpu.SemaphoreType.DMA((4,))]
    layer_two, layer_one = call(widen_own_kernel, outs, [VMEM], terms, out_specs=(ANY, ANY), scratch_shapes=scratch)
    layer_two, layer_one = call(
        widen_recv_kernel,
        outs,
        [VMEM, ANY, ANY],
        recv,
        layer_two,
        layer_one,
        out_specs=(ANY, ANY),
        scratch_shapes=scratch,
        input_output_aliases={1: 0, 2: 1},
    )
    return layer_two.reshape(2, 256, 256), layer_one.reshape(2, 768, 256)


def solution(mesh):
    fine = jax.sharding.Mesh(mesh.devices.reshape(4, 2, 2, 2, 4, 2, 2), ROW + COL)
    row, col = ROW, COL
    in_specs = (
        P(col, row, None),
        P(col, row, None),
        P(col, row, None),
        P(col, row, None),
        P(),
        P(),
        P(row, col, None, None, None),
        P(row, col, None),
        P(row, col),
        P(col, None),
        P(row, col, None),
        P(row, col, None),
        P(row, col, None),
    )
    out_specs = (P(), P())
    return jax.shard_map(local, mesh=fine, in_specs=in_specs, out_specs=out_specs, check_vma=False)
```

time: 744 us -> 123 us (0.17)
  waiting for transfers between devices: 585 us -> 20.9 us
  blocking collectives: 113 us -> 44.9 us
  starting transfers between devices: 0.08 us -> 42.7 us
  other arithmetic: 16.6 us -> 0.19 us
  between operations: 14.9 us -> 1.52 us
  Pallas kernels: 0 us -> 8.36 us
    psum x1 -> x0, waiting for transfers between devices: 472 us -> none  [local(): layer_two, layer_one = lax.psum((two_terms, one_terms), ('row', 'col'))]
    all_gather x1 -> x0, blocking collectives: 113 us -> none  [local(): gathered = lax.all_gather(delta_two, 'row', axis=0, tiled=True)]
    reduce_scatter x1 -> x0, waiting for transfers between devices: 113 us -> none  [local(): lax.psum_scatter(partial_value.astype(jnp.bfloat16), 'col', scatter_dimen...]
    all_to_all x0 -> x3, blocking collectives: none -> 44.9 us  [exchange(): return lax.all_to_all(blocks, axes, 0, 0, tiled=True)]
    ppermute x0 -> x4, starting transfers between devices: none -> 22.6 us  [swap(): return lax.ppermute(value, axis, [(0, 1), (1, 0)])]
    all_to_all x0 -> x2, starting transfers between devices: none -> 20.1 us  [exchange(): return lax.all_to_all(blocks, axes, 0, 0, tiled=True)]
    all_to_all x0 -> x2, waiting for transfers between devices: none -> 11.7 us  [exchange(): return lax.all_to_all(blocks, axes, 0, 0, tiled=True)]
    ppermute x0 -> x4, waiting for transfers between devices: none -> 9.2 us  [swap(): return lax.ppermute(value, axis, [(0, 1), (1, 0)])]
  transfers between devices with their start and end apart: 2 -> 6, of which waited for: 2 -> 5; matrix products, arithmetic and copies ran while one was open for 0% -> 0% of each run, Pallas kernels for 0% -> 3%
where the time goes in v1:
time: 123 us
  blocking collectives  44.9 us (37%)
  starting transfers between devices  42.7 us (35%)
  waiting for transfers between devices  20.9 us (17%)
  Pallas kernels  8.36 us (7%)
  local copies, waits for them, and re-layouts  4.39 us (4%)
  between operations  1.52 us (1%)
    all_to_all x3, blocking collectives, exchange(): return lax.all_to_all(blocks, axes, 0, 0, tiled=True)  44.9 us
    ppermute x4, starting transfers between devices, swap(): return lax.ppermute(value, axis, [(0, 1), (1, 0)])  22.6 us
    all_to_all x2, starting transfers between devices, exchange(): return lax.all_to_all(blocks, axes, 0, 0, tiled=True)  20.1 us
    all_to_all x2, waiting for transfers between devices, exchange(): return lax.all_to_all(blocks, axes, 0, 0, tiled=True)  11.7 us
    ppermute x4, waiting for transfers between devices, swap(): return lax.ppermute(value, axis, [(0, 1), (1, 0)])  9.2 us
    pallas_call x10, Pallas kernels, call(): pl.pallas_call(kernel, out_shape=outs, in_specs=ins, compiler_params=pltp...  8.36 us
    unnamed x24, local copies, waits for them, and re-layouts  4.22 us
  transfers between devices with their start and end apart: 6, of which 5 were waited for; matrix products, arithmetic and copies ran while one was open for 0% of the time, Pallas kernels for 3%

profile of v1, /device:TPU:1, one launch (start us, length us, event | category | flops | bytes accessed | tf_op | source)
XLA Modules:
  0.0 122.9 jit_solution(6128767571515473751)
XLA Ops:
  0.6 1.4 %mask.1 = bf16[32,8,256]{2,1,0:T(8,128)(2,1)} custom-call(bf16[8,256]{1,0:T(8,128)(2,1)} %bitcast.33, bf16[8,256]{1,0:T(8,128)(2,1)} %bitcast.35), custom_call_target="tpu_custom_call" | custom-call | flops 10000 | bytes 140000 | tf_op jit(solution)/shard_map/mask/pallas_call | solution.py:161
  2.0 16.1 %all-to-all-start = ((bf16[32,8,256]{2,1,0:T(8,128)(2,1)}), bf16[32,8,256]{2,1,0:T(8,128)(2,1)S(1)}, u32[]{:S(2)}, u32[]{:S(2)}) async-start(bf16[32,8,256]{2,1,0:T(8,128)(2,1)} %mask.1), calls=%async_computation | async-start | bytes 262144 | tf_op jit(solution)/shard_map/all_to_all | solution.py:20
  18.8 0.0 copy-start
  18.8 1.0 copy-done
  19.8 0.9 copy-done.3
  20.7 0.9 copy-done.4
  21.6 0.7 copy-done.10
  22.3 0.7 copy-done.11
  23.0 1.5 %layout.1 = (bf16[16,128,512]{2,1,0:T(8,128)(2,1)S(1)}, bf16[2,256,256]{2,1,0:T(8,128)(2,1)S(1)}) custom-call(s32[1,16]{1,0:T(1,128)S(1)} %bitcast.39, s32[1,1]{1,0:T(1,128)S(6)} %copy.19.count_ref, bf16[16,128,128]{2,1,0:T(8,128)(2,1)S(1)} %bitcast.29, s32[1,256]{1,0:T(1,128)S(1)} %copy-done.10, bf16[256,256]{1,0:T(8,128)(2,1)S(1)} %copy-done.3, ...), custom_call_target="tpu_custom_call" | custom-call | flops 1000000 | bytes 3000000 | tf_op jit(solution)/shard_map/layout/pallas_call | solution.py:161
  24.5 5.4 %all-to-all-done = bf16[32,8,256]{2,1,0:T(8,128)(2,1)S(1)} async-done(((bf16[32,8,256]{2,1,0:T(8,128)(2,1)}), bf16[32,8,256]{2,1,0:T(8,128)(2,1)S(1)}, u32[]{:S(2)}, u32[]{:S(2)}) %all-to-all-start) | async-done | bytes 131104 | tf_op jit(solution)/shard_map/all_to_all | solution.py:20
  29.9 0.9 send.1
  30.8 5.4 %collective-permute-start = (bf16[2048,128]{1,0:T(8,128)(2,1)S(1)}, bf16[2048,128]{1,0:T(8,128)(2,1)S(1)}, u32[]{:S(2)}, u32[]{:S(2)}) collective-permute-start(bf16[2048,128]{1,0:T(8,128)(2,1)S(1)} %send.1), channel_id=1, source_target_pairs={{0,1},{1,0},{2,3},{3,2},{4,5},{5,4},{6,7},{7,6},{8,9},{9,8},{10,11... | collective-permute-start | bytes 1572872 | tf_op jit(solution)/shard_map/ppermute | solution.py:28
  36.3 0.9 keep.1.keep_ref
  37.3 0.5 collective-permute-done.recv_ref
  37.8 0.9 pair.1
  38.7 4.0 %all-to-all-start.1 = ((bf16[4,2,256,128]{3,2,1,0:T(8,128)(2,1)}), bf16[4,2,256,128]{3,2,1,0:T(8,128)(2,1)S(1)}, u32[]{:S(2)}, u32[]{:S(2)}) async-start(bf16[4,2,256,128]{3,2,1,0:T(8,128)(2,1)} %bitcast.6), calls=%async_computation.1 | async-start | bytes 1048576 | tf_op jit(solution)/shard_map/all_to_all | solution.py:20
  42.8 2.6 %collective-permute-start.2 = (bf16[144,1792]{1,0:T(8,128)(2,1)S(1)}, bf16[144,1792]{1,0:T(8,128)(2,1)S(1)}, u32[]{:S(2)}, u32[]{:S(2)}) collective-permute-start(bf16[144,1792]{1,0:T(8,128)(2,1)S(1)} %bundle.1.own_ref), channel_id=1, source_target_pairs={{0,1},{1,0},{2,3},{3,2},{4,5},{5,4},{6,7},{7,6},{8,9},{9,8},{10,11... | collective-permute-start | bytes 1548296 | tf_op jit(solution)/shard_map/ppermute | solution.py:28
  45.3 6.2 %all-to-all-done.1 = bf16[4,2,256,128]{3,2,1,0:T(8,128)(2,1)S(1)} async-done(((bf16[4,2,256,128]{3,2,1,0:T(8,128)(2,1)}), bf16[4,2,256,128]{3,2,1,0:T(8,128)(2,1)S(1)}, u32[]{:S(2)}, u32[]{:S(2)}) %all-to-all-start.1) | async-done | bytes 524320 | tf_op jit(solution)/shard_map/all_to_all | solution.py:20
  51.6 0.1 convert_reduce_fusion
  51.7 7.9 %collective-permute-start.1 = (bf16[256,128]{1,0:T(8,128)(2,1)S(1)}, bf16[256,128]{1,0:T(8,128)(2,1)S(1)}, u32[]{:S(2)}, u32[]{:S(2)}) collective-permute-start(bf16[256,128]{1,0:T(8,128)(2,1)S(1)} %fusion), channel_id=1, source_target_pairs={{0,2},{2,0},{1,3},{3,1},{4,6},{6,4},{5,7},{7,5},{8,10},{10,8},{9,1... | collective-permute-start | bytes 196616 | tf_op jit(solution)/shard_map/ppermute | solution.py:28
  59.7 0.4 turn.1
  60.0 8.2 %collective-permute-done.1.recv_ref = bf16[256,128]{1,0:T(8,128)(2,1)S(1)} collective-permute-done((bf16[256,128]{1,0:T(8,128)(2,1)S(1)}, bf16[256,128]{1,0:T(8,128)(2,1)S(1)}, u32[]{:S(2)}, u32[]{:S(2)}) %collective-permute-start.1) | collective-permute-done | bytes 65568 | tf_op jit(solution)/shard_map/ppermute | solution.py:28
  68.2 0.4 terms.1
  68.6 12.8 %all_to_all.25 = bf16[32,64,128]{2,1,0:T(8,128)(2,1)S(1)} all-to-all(bf16[32,64,128]{2,1,0:T(8,128)(2,1)S(1)} %bitcast.26), channel_id=1, replica_groups=mesh['y'=4,'zm'=2,'zna'=2,'znb'=2,'x'=4,'zh'=2,'core'=2] {'znb','y','x'}, dimensions={0} | all-to-all | bytes 1048576 | tf_op jit(solution)/shard_map/all_to_all | solution.py:20
  81.4 0.1 reduce_sum.34
  81.5 18.3 %all_to_all.26 = bf16[8,64,128]{2,1,0:T(8,128)(2,1)S(1)} all-to-all(bf16[8,64,128]{2,1,0:T(8,128)(2,1)S(1)} %broadcast_in_dim.4), channel_id=1, replica_groups=mesh['y'=4,'zm'=2,'zna'=2,'znb'=2,'x'=4,'zh'=2,'core'=2] {'zna','zm','zh'}, dimensions={0} | all-to-all | bytes 262144 | tf_op jit(solution)/shard_map/all_to_all | solution.py:20
  99.8 0.1 broadcast_in_dim.5
  100.0 13.7 %all_to_all.27 = bf16[32,64,128]{2,1,0:T(8,128)(2,1)S(1)} all-to-all(bf16[32,64,128]{2,1,0:T(8,128)(2,1)S(1)} %broadcast_in_dim.5), channel_id=1, replica_groups=mesh['y'=4,'zm'=2,'zna'=2,'znb'=2,'x'=4,'zh'=2,'core'=2] {'znb','y','x'}, dimensions={0} | all-to-all | bytes 1048576 | tf_op jit(solution)/shard_map/all_to_all | solution.py:20
  113.7 6.7 %collective-permute-start.3 = (bf16[2048,128]{1,0:T(8,128)(2,1)S(1)}, bf16[2048,128]{1,0:T(8,128)(2,1)S(1)}, u32[]{:S(2)}, u32[]{:S(2)}) collective-permute-start(bf16[2048,128]{1,0:T(8,128)(2,1)S(1)} %bitcast.24), channel_id=1, source_target_pairs={{0,1},{1,0},{2,3},{3,2},{4,5},{5,4},{6,7},{7,6},{8,9},{9,8},{10,11... | collective-permute-start | bytes 1572872 | tf_op jit(solution)/shard_map/ppermute | solution.py:28
  120.4 1.0 widen_own.1
  121.4 0.5 collective-permute-done.3.recv_ref
  121.9 1.0 widen_recv.1
  (24 shorter events, 0.2 us)
Async XLA Ops:
  2.0 27.9 %all-to-all-start = ((bf16[32,8,256]{2,1,0:T(8,128)(2,1)}), bf16[32,8,256]{2,1,0:T(8,128)(2,1)S(1)}, u32[]{:S(2)}, u32[]{:S(2)}) async-start(bf16[32,8,256]{2,1,0:T(8,128)(2,1)} %mask.1), calls=%async_computation | async-start | bytes 262144 | tf_op jit(solution)/shard_map/all_to_all | solution.py:20
  18.8 1.0 copy-start
  19.8 0.9 copy-start.3
  20.7 0.9 copy-start.4
  21.6 0.7 copy-start.10
  22.3 0.7 copy-start.11
  30.8 7.0 %collective-permute-start = (bf16[2048,128]{1,0:T(8,128)(2,1)S(1)}, bf16[2048,128]{1,0:T(8,128)(2,1)S(1)}, u32[]{:S(2)}, u32[]{:S(2)}) collective-permute-start(bf16[2048,128]{1,0:T(8,128)(2,1)S(1)} %send.1), channel_id=1, source_target_pairs={{0,1},{1,0},{2,3},{3,2},{4,5},{5,4},{6,7},{7,6},{8,9},{9,8},{10,11... | collective-permute-start | bytes 1572872 | tf_op jit(solution)/shard_map/ppermute | solution.py:28
  37.2 5.5 %copy-start.1 = (bf16[1,128,768]{2,1,0:T(8,128)(2,1)S(1)}, bf16[1,128,768]{2,1,0:T(8,128)(2,1)}, u32[]{:S(2)}) copy-start(bf16[1,128,768]{2,1,0:T(8,128)(2,1)} %param.24) | copy-start | bytes 589828
  37.2 5.5 %copy-start.2 = (bf16[1,128,768]{2,1,0:T(8,128)(2,1)S(1)}, bf16[1,128,768]{2,1,0:T(8,128)(2,1)}, u32[]{:S(2)}) copy-start(bf16[1,128,768]{2,1,0:T(8,128)(2,1)} %param.25) | copy-start | bytes 589828
  37.2 5.5 %copy-start.5 = (bf16[1,128,256]{2,1,0:T(8,128)(2,1)S(1)}, bf16[1,128,256]{2,1,0:T(8,128)(2,1)}, u32[]{:S(2)}) copy-start(bf16[1,128,256]{2,1,0:T(8,128)(2,1)} %param.23) | copy-start | bytes 196612
  37.2 5.5 %copy-start.6 = (bf16[1,8,256]{2,1,0:T(8,128)(2,1)S(1)}, bf16[1,8,256]{2,1,0:T(8,128)(2,1)}, u32[]{:S(2)}) copy-start(bf16[1,8,256]{2,1,0:T(8,128)(2,1)} %param.13) | copy-start | bytes 12292
  37.2 5.5 %copy-start.7 = (bf16[1,8,256]{2,1,0:T(8,128)(2,1)S(1)}, bf16[1,8,256]{2,1,0:T(8,128)(2,1)}, u32[]{:S(2)}) copy-start(bf16[1,8,256]{2,1,0:T(8,128)(2,1)} %param.14) | copy-start | bytes 12292
  37.2 5.5 %copy-start.8 = (bf16[1,8,256]{2,1,0:T(8,128)(2,1)S(1)}, bf16[1,8,256]{2,1,0:T(8,128)(2,1)}, u32[]{:S(2)}) copy-start(bf16[1,8,256]{2,1,0:T(8,128)(2,1)} %param.15) | copy-start | bytes 12292
  37.3 5.5 %copy-start.9 = (bf16[1,8,256]{2,1,0:T(8,128)(2,1)S(1)}, bf16[1,8,256]{2,1,0:T(8,128)(2,1)}, u32[]{:S(2)}) copy-start(bf16[1,8,256]{2,1,0:T(8,128)(2,1)} %param.16) | copy-start | bytes 12292
  38.7 12.9 %all-to-all-start.1 = ((bf16[4,2,256,128]{3,2,1,0:T(8,128)(2,1)}), bf16[4,2,256,128]{3,2,1,0:T(8,128)(2,1)S(1)}, u32[]{:S(2)}, u32[]{:S(2)}) async-start(bf16[4,2,256,128]{3,2,1,0:T(8,128)(2,1)} %bitcast.6), calls=%async_computation.1 | async-start | bytes 1048576 | tf_op jit(solution)/shard_map/all_to_all | solution.py:20
  42.8 16.9 %collective-permute-start.2 = (bf16[144,1792]{1,0:T(8,128)(2,1)S(1)}, bf16[144,1792]{1,0:T(8,128)(2,1)S(1)}, u32[]{:S(2)}, u32[]{:S(2)}) collective-permute-start(bf16[144,1792]{1,0:T(8,128)(2,1)S(1)} %bundle.1.own_ref), channel_id=1, source_target_pairs={{0,1},{1,0},{2,3},{3,2},{4,5},{5,4},{6,7},{7,6},{8,9},{9,8},{10,11... | collective-permute-start | bytes 1548296 | tf_op jit(solution)/shard_map/ppermute | solution.py:28
  51.7 16.5 %collective-permute-start.1 = (bf16[256,128]{1,0:T(8,128)(2,1)S(1)}, bf16[256,128]{1,0:T(8,128)(2,1)S(1)}, u32[]{:S(2)}, u32[]{:S(2)}) collective-permute-start(bf16[256,128]{1,0:T(8,128)(2,1)S(1)} %fusion), channel_id=1, source_target_pairs={{0,2},{2,0},{1,3},{3,1},{4,6},{6,4},{5,7},{7,5},{8,10},{10,8},{9,1... | collective-permute-start | bytes 196616 | tf_op jit(solution)/shard_map/ppermute | solution.py:28
  113.7 8.2 %collective-permute-start.3 = (bf16[2048,128]{1,0:T(8,128)(2,1)S(1)}, bf16[2048,128]{1,0:T(8,128)(2,1)S(1)}, u32[]{:S(2)}, u32[]{:S(2)}) collective-permute-start(bf16[2048,128]{1,0:T(8,128)(2,1)S(1)} %bitcast.24), channel_id=1, source_target_pairs={{0,1},{1,0},{2,3},{3,2},{4,5},{5,4},{6,7},{7,6},{8,9},{9,8},{10,11... | collective-permute-start | bytes 1572872 | tf_op jit(solution)/shard_map/ppermute | solution.py:28

commit v2 on v1

--- a/solution.py
+++ b/solution.py
@@ -102,6 +102,12 @@
     by_core(body)
 
 
+def by_rows(start, count, body, step=128):
+    @pl.loop(0, count // step)
+    def _(turn):
+        body(pl.ds(pl.multiple_of(start + turn * step, step), step))
+
+
 def product(delta_ref, weight_ref, layout_ref, columns):
     delta = delta_ref[...]
     message = [dot(delta, weight_ref[at, columns], LAST_BOTH).astype(jnp.bfloat16) for at in range(2)]
@@ -123,7 +129,10 @@
 
 
 def pair_kernel(keep_ref, recv_ref, sum_ref):
-    sum_ref[...] = (keep_ref[...] + recv_ref[...].astype(jnp.float32)).astype(jnp.bfloat16)
+    def add(rows):
+        sum_ref[rows] = (keep_ref[rows] + recv_ref[rows].astype(jnp.float32)).astype(jnp.bfloat16)
+
+    by_rows(0, 2048, add)
 
 
 def terms_kernel(keep_ref, recv_ref, preact_ref, turned_ref, two_ref, terms_ref):
@@ -139,7 +148,11 @@
         rows = pl.ds(turn * 512, 512)
         target = one_ref.at[rows, columns] if turn < 3 else two_ref.at[:, columns]
         copies.append(pltpu.make_async_copy(wide.at[rows], target, sems.at[turn]))
-        wide[rows] = value_ref[rows].astype(jnp.float32)
+
+        def convert(part):
+            wide[part] = value_ref[part].astype(jnp.float32)
+
+        by_rows(turn * 512, 512, convert)
         copies[-1].start()
     for copy in copies:
         copy.wait()

time: 123 us -> 124 us (level)
  no operation moved by 1% of the time
where the time goes in v2:
time: 124 us; the launch traced here: 123 us
  blocking collectives  44.9 us (36%)
  starting transfers between devices  42.7 us (34%)
  waiting for transfers between devices  21.1 us (17%)
  Pallas kernels  8.22 us (7%)
  local copies, waits for them, and re-layouts  4.39 us (4%)
  between operations  1.52 us (1%)
    all_to_all x3, blocking collectives, exchange(): return lax.all_to_all(blocks, axes, 0, 0, tiled=True)  44.9 us
    ppermute x4, starting transfers between devices, swap(): return lax.ppermute(value, axis, [(0, 1), (1, 0)])  22.6 us
    all_to_all x2, starting transfers between devices, exchange(): return lax.all_to_all(blocks, axes, 0, 0, tiled=True)  20.1 us
    all_to_all x2, waiting for transfers between devices, exchange(): return lax.all_to_all(blocks, axes, 0, 0, tiled=True)  11.9 us
    ppermute x4, waiting for transfers between devices, swap(): return lax.ppermute(value, axis, [(0, 1), (1, 0)])  9.18 us
    pallas_call x10, Pallas kernels, call(): pl.pallas_call(kernel, out_shape=outs, in_specs=ins, compiler_params=pltp...  8.22 us
    unnamed x24, local copies, waits for them, and re-layouts  4.22 us
  transfers between devices with their start and end apart: 6, of which 5 were waited for; matrix products, arithmetic and copies ran while one was open for 0% of the time, Pallas kernels for 3%

profile of v2, /device:TPU:1, one launch (start us, length us, event | category | flops | bytes accessed | tf_op | source)
XLA Modules:
  0.0 123.0 jit_solution(4730492968583153668)
XLA Ops:
  0.6 1.4 %mask.1 = bf16[32,8,256]{2,1,0:T(8,128)(2,1)} custom-call(bf16[8,256]{1,0:T(8,128)(2,1)} %bitcast.33, bf16[8,256]{1,0:T(8,128)(2,1)} %bitcast.35), custom_call_target="tpu_custom_call" | custom-call | flops 10000 | bytes 140000 | tf_op jit(solution)/shard_map/mask/pallas_call | solution.py:174
  2.0 16.1 %all-to-all-start = ((bf16[32,8,256]{2,1,0:T(8,128)(2,1)}), bf16[32,8,256]{2,1,0:T(8,128)(2,1)S(1)}, u32[]{:S(2)}, u32[]{:S(2)}) async-start(bf16[32,8,256]{2,1,0:T(8,128)(2,1)} %mask.1), calls=%async_computation | async-start | bytes 262144 | tf_op jit(solution)/shard_map/all_to_all | solution.py:20
  18.8 0.0 copy-start
  18.8 1.0 copy-done
  19.8 0.9 copy-done.3
  20.7 0.9 copy-done.4
  21.6 0.7 copy-done.10
  22.3 0.7 copy-done.11
  23.0 1.3 %layout.1 = (bf16[16,128,512]{2,1,0:T(8,128)(2,1)S(1)}, bf16[2,256,256]{2,1,0:T(8,128)(2,1)S(1)}) custom-call(s32[1,16]{1,0:T(1,128)S(1)} %bitcast.39, s32[1,1]{1,0:T(1,128)S(6)} %copy.19.count_ref, bf16[16,128,128]{2,1,0:T(8,128)(2,1)S(1)} %bitcast.29, s32[1,256]{1,0:T(1,128)S(1)} %copy-done.10, bf16[256,256]{1,0:T(8,128)(2,1)S(1)} %copy-done.3, ...), custom_call_target="tpu_custom_call" | custom-call | flops 1000000 | bytes 3000000 | tf_op jit(solution)/shard_map/layout/pallas_call | solution.py:174
  24.2 5.7 %all-to-all-done = bf16[32,8,256]{2,1,0:T(8,128)(2,1)S(1)} async-done(((bf16[32,8,256]{2,1,0:T(8,128)(2,1)}), bf16[32,8,256]{2,1,0:T(8,128)(2,1)S(1)}, u32[]{:S(2)}, u32[]{:S(2)}) %all-to-all-start) | async-done | bytes 131104 | tf_op jit(solution)/shard_map/all_to_all | solution.py:20
  29.9 0.9 send.1
  30.8 5.4 %collective-permute-start = (bf16[2048,128]{1,0:T(8,128)(2,1)S(1)}, bf16[2048,128]{1,0:T(8,128)(2,1)S(1)}, u32[]{:S(2)}, u32[]{:S(2)}) collective-permute-start(bf16[2048,128]{1,0:T(8,128)(2,1)S(1)} %send.1), channel_id=1, source_target_pairs={{0,1},{1,0},{2,3},{3,2},{4,5},{5,4},{6,7},{7,6},{8,9},{9,8},{10,11... | collective-permute-start | bytes 1572872 | tf_op jit(solution)/shard_map/ppermute | solution.py:28
  36.3 0.9 keep.1.keep_ref
  37.3 0.5 collective-permute-done.recv_ref
  37.8 0.9 pair.1
  38.7 4.0 %all-to-all-start.1 = ((bf16[4,2,256,128]{3,2,1,0:T(8,128)(2,1)}), bf16[4,2,256,128]{3,2,1,0:T(8,128)(2,1)S(1)}, u32[]{:S(2)}, u32[]{:S(2)}) async-start(bf16[4,2,256,128]{3,2,1,0:T(8,128)(2,1)} %bitcast.6), calls=%async_computation.1 | async-start | bytes 1048576 | tf_op jit(solution)/shard_map/all_to_all | solution.py:20
  42.8 2.6 %collective-permute-start.2 = (bf16[144,1792]{1,0:T(8,128)(2,1)S(1)}, bf16[144,1792]{1,0:T(8,128)(2,1)S(1)}, u32[]{:S(2)}, u32[]{:S(2)}) collective-permute-start(bf16[144,1792]{1,0:T(8,128)(2,1)S(1)} %bundle.1.own_ref), channel_id=1, source_target_pairs={{0,1},{1,0},{2,3},{3,2},{4,5},{5,4},{6,7},{7,6},{8,9},{9,8},{10,11... | collective-permute-start | bytes 1548296 | tf_op jit(solution)/shard_map/ppermute | solution.py:28
  45.4 6.2 %all-to-all-done.1 = bf16[4,2,256,128]{3,2,1,0:T(8,128)(2,1)S(1)} async-done(((bf16[4,2,256,128]{3,2,1,0:T(8,128)(2,1)}), bf16[4,2,256,128]{3,2,1,0:T(8,128)(2,1)S(1)}, u32[]{:S(2)}, u32[]{:S(2)}) %all-to-all-start.1) | async-done | bytes 524320 | tf_op jit(solution)/shard_map/all_to_all | solution.py:20
  51.6 0.1 convert_reduce_fusion
  51.7 7.9 %collective-permute-start.1 = (bf16[256,128]{1,0:T(8,128)(2,1)S(1)}, bf16[256,128]{1,0:T(8,128)(2,1)S(1)}, u32[]{:S(2)}, u32[]{:S(2)}) collective-permute-start(bf16[256,128]{1,0:T(8,128)(2,1)S(1)} %fusion), channel_id=1, source_target_pairs={{0,2},{2,0},{1,3},{3,1},{4,6},{6,4},{5,7},{7,5},{8,10},{10,8},{9,1... | collective-permute-start | bytes 196616 | tf_op jit(solution)/shard_map/ppermute | solution.py:28
  59.7 0.4 turn.1
  60.1 8.2 %collective-permute-done.1.recv_ref = bf16[256,128]{1,0:T(8,128)(2,1)S(1)} collective-permute-done((bf16[256,128]{1,0:T(8,128)(2,1)S(1)}, bf16[256,128]{1,0:T(8,128)(2,1)S(1)}, u32[]{:S(2)}, u32[]{:S(2)}) %collective-permute-start.1) | collective-permute-done | bytes 65568 | tf_op jit(solution)/shard_map/ppermute | solution.py:28
  68.3 0.4 terms.1
  68.7 12.8 %all_to_all.25 = bf16[32,64,128]{2,1,0:T(8,128)(2,1)S(1)} all-to-all(bf16[32,64,128]{2,1,0:T(8,128)(2,1)S(1)} %bitcast.26), channel_id=1, replica_groups=mesh['y'=4,'zm'=2,'zna'=2,'znb'=2,'x'=4,'zh'=2,'core'=2] {'znb','y','x'}, dimensions={0} | all-to-all | bytes 1048576 | tf_op jit(solution)/shard_map/all_to_all | solution.py:20
  81.5 0.1 reduce_sum.34
  81.6 18.3 %all_to_all.26 = bf16[8,64,128]{2,1,0:T(8,128)(2,1)S(1)} all-to-all(bf16[8,64,128]{2,1,0:T(8,128)(2,1)S(1)} %broadcast_in_dim.4), channel_id=1, replica_groups=mesh['y'=4,'zm'=2,'zna'=2,'znb'=2,'x'=4,'zh'=2,'core'=2] {'zna','zm','zh'}, dimensions={0} | all-to-all | bytes 262144 | tf_op jit(solution)/shard_map/all_to_all | solution.py:20
  99.9 0.1 broadcast_in_dim.5
  100.0 13.7 %all_to_all.27 = bf16[32,64,128]{2,1,0:T(8,128)(2,1)S(1)} all-to-all(bf16[32,64,128]{2,1,0:T(8,128)(2,1)S(1)} %broadcast_in_dim.5), channel_id=1, replica_groups=mesh['y'=4,'zm'=2,'zna'=2,'znb'=2,'x'=4,'zh'=2,'core'=2] {'znb','y','x'}, dimensions={0} | all-to-all | bytes 1048576 | tf_op jit(solution)/shard_map/all_to_all | solution.py:20
  113.8 6.7 %collective-permute-start.3 = (bf16[2048,128]{1,0:T(8,128)(2,1)S(1)}, bf16[2048,128]{1,0:T(8,128)(2,1)S(1)}, u32[]{:S(2)}, u32[]{:S(2)}) collective-permute-start(bf16[2048,128]{1,0:T(8,128)(2,1)S(1)} %bitcast.24), channel_id=1, source_target_pairs={{0,1},{1,0},{2,3},{3,2},{4,5},{5,4},{6,7},{7,6},{8,9},{9,8},{10,11... | collective-permute-start | bytes 1572872 | tf_op jit(solution)/shard_map/ppermute | solution.py:28
  120.4 1.0 widen_own.1
  121.5 0.5 collective-permute-done.3.recv_ref
  122.0 1.0 widen_recv.1
  (24 shorter events, 0.2 us)
Async XLA Ops:
  2.0 27.9 %all-to-all-start = ((bf16[32,8,256]{2,1,0:T(8,128)(2,1)}), bf16[32,8,256]{2,1,0:T(8,128)(2,1)S(1)}, u32[]{:S(2)}, u32[]{:S(2)}) async-start(bf16[32,8,256]{2,1,0:T(8,128)(2,1)} %mask.1), calls=%async_computation | async-start | bytes 262144 | tf_op jit(solution)/shard_map/all_to_all | solution.py:20
  18.8 1.0 copy-start
  19.8 0.9 copy-start.3
  20.7 0.9 copy-start.4
  21.6 0.7 copy-start.10
  22.3 0.7 copy-start.11
  30.8 7.0 %collective-permute-start = (bf16[2048,128]{1,0:T(8,128)(2,1)S(1)}, bf16[2048,128]{1,0:T(8,128)(2,1)S(1)}, u32[]{:S(2)}, u32[]{:S(2)}) collective-permute-start(bf16[2048,128]{1,0:T(8,128)(2,1)S(1)} %send.1), channel_id=1, source_target_pairs={{0,1},{1,0},{2,3},{3,2},{4,5},{5,4},{6,7},{7,6},{8,9},{9,8},{10,11... | collective-permute-start | bytes 1572872 | tf_op jit(solution)/shard_map/ppermute | solution.py:28
  37.2 5.6 %copy-start.1 = (bf16[1,128,768]{2,1,0:T(8,128)(2,1)S(1)}, bf16[1,128,768]{2,1,0:T(8,128)(2,1)}, u32[]{:S(2)}) copy-start(bf16[1,128,768]{2,1,0:T(8,128)(2,1)} %param.24) | copy-start | bytes 589828
  37.2 5.6 %copy-start.2 = (bf16[1,128,768]{2,1,0:T(8,128)(2,1)S(1)}, bf16[1,128,768]{2,1,0:T(8,128)(2,1)}, u32[]{:S(2)}) copy-start(bf16[1,128,768]{2,1,0:T(8,128)(2,1)} %param.25) | copy-start | bytes 589828
  37.2 5.5 %copy-start.5 = (bf16[1,128,256]{2,1,0:T(8,128)(2,1)S(1)}, bf16[1,128,256]{2,1,0:T(8,128)(2,1)}, u32[]{:S(2)}) copy-start(bf16[1,128,256]{2,1,0:T(8,128)(2,1)} %param.23) | copy-start | bytes 196612
  37.2 5.5 %copy-start.6 = (bf16[1,8,256]{2,1,0:T(8,128)(2,1)S(1)}, bf16[1,8,256]{2,1,0:T(8,128)(2,1)}, u32[]{:S(2)}) copy-start(bf16[1,8,256]{2,1,0:T(8,128)(2,1)} %param.13) | copy-start | bytes 12292
  37.2 5.5 %copy-start.7 = (bf16[1,8,256]{2,1,0:T(8,128)(2,1)S(1)}, bf16[1,8,256]{2,1,0:T(8,128)(2,1)}, u32[]{:S(2)}) copy-start(bf16[1,8,256]{2,1,0:T(8,128)(2,1)} %param.14) | copy-start | bytes 12292
  37.2 5.5 %copy-start.8 = (bf16[1,8,256]{2,1,0:T(8,128)(2,1)S(1)}, bf16[1,8,256]{2,1,0:T(8,128)(2,1)}, u32[]{:S(2)}) copy-start(bf16[1,8,256]{2,1,0:T(8,128)(2,1)} %param.15) | copy-start | bytes 12292
  37.3 5.5 %copy-start.9 = (bf16[1,8,256]{2,1,0:T(8,128)(2,1)S(1)}, bf16[1,8,256]{2,1,0:T(8,128)(2,1)}, u32[]{:S(2)}) copy-start(bf16[1,8,256]{2,1,0:T(8,128)(2,1)} %param.16) | copy-start | bytes 12292
  38.7 12.9 %all-to-all-start.1 = ((bf16[4,2,256,128]{3,2,1,0:T(8,128)(2,1)}), bf16[4,2,256,128]{3,2,1,0:T(8,128)(2,1)S(1)}, u32[]{:S(2)}, u32[]{:S(2)}) async-start(bf16[4,2,256,128]{3,2,1,0:T(8,128)(2,1)} %bitcast.6), calls=%async_computation.1 | async-start | bytes 1048576 | tf_op jit(solution)/shard_map/all_to_all | solution.py:20
  42.8 16.9 %collective-permute-start.2 = (bf16[144,1792]{1,0:T(8,128)(2,1)S(1)}, bf16[144,1792]{1,0:T(8,128)(2,1)S(1)}, u32[]{:S(2)}, u32[]{:S(2)}) collective-permute-start(bf16[144,1792]{1,0:T(8,128)(2,1)S(1)} %bundle.1.own_ref), channel_id=1, source_target_pairs={{0,1},{1,0},{2,3},{3,2},{4,5},{5,4},{6,7},{7,6},{8,9},{9,8},{10,11... | collective-permute-start | bytes 1548296 | tf_op jit(solution)/shard_map/ppermute | solution.py:28
  51.7 16.5 %collective-permute-start.1 = (bf16[256,128]{1,0:T(8,128)(2,1)S(1)}, bf16[256,128]{1,0:T(8,128)(2,1)S(1)}, u32[]{:S(2)}, u32[]{:S(2)}) collective-permute-start(bf16[256,128]{1,0:T(8,128)(2,1)S(1)} %fusion), channel_id=1, source_target_pairs={{0,2},{2,0},{1,3},{3,1},{4,6},{6,4},{5,7},{7,5},{8,10},{10,8},{9,1... | collective-permute-start | bytes 196616 | tf_op jit(solution)/shard_map/ppermute | solution.py:28
  113.8 8.2 %collective-permute-start.3 = (bf16[2048,128]{1,0:T(8,128)(2,1)S(1)}, bf16[2048,128]{1,0:T(8,128)(2,1)S(1)}, u32[]{:S(2)}, u32[]{:S(2)}) collective-permute-start(bf16[2048,128]{1,0:T(8,128)(2,1)S(1)} %bitcast.24), channel_id=1, source_target_pairs={{0,1},{1,0},{2,3},{3,2},{4,5},{5,4},{6,7},{7,6},{8,9},{9,8},{10,11... | collective-permute-start | bytes 1572872 | tf_op jit(solution)/shard_map/ppermute | solution.py:28

commit v3 on v2

--- a/solution.py
+++ b/solution.py
@@ -108,8 +108,14 @@
         body(pl.ds(pl.multiple_of(start + turn * step, step), step))
 
 
+def natural_order():
+    for row in range(32):
+        y, zm, zna, znb = row // 8, row // 4 % 2, row // 2 % 2, row % 2
+        yield ((y * 2 + znb) * 2 + zna) * 2 + zm
+
+
 def product(delta_ref, weight_ref, layout_ref, columns):
-    delta = delta_ref[...]
+    delta = jnp.concatenate([delta_ref[at].astype(jnp.float32) for at in natural_order()]).astype(jnp.bfloat16)
     message = [dot(delta, weight_ref[at, columns], LAST_BOTH).astype(jnp.bfloat16) for at in range(2)]
     return dot(layout_ref[...], jnp.concatenate(message))
 
@@ -210,7 +216,7 @@
         out_specs=VMEM,
         scratch_shapes=[pltpu.VMEM((2, 8, 256), jnp.bfloat16), pltpu.SemaphoreType.DMA((2,))],
     )
-    gathered = exchange(copies, ROW).reshape(256, 256)
+    gathered = exchange(copies, ("y", "znb", "zna", "zm"))
     layout, weight = call(
         layout_kernel,
         (shape((16, 128, 512)), shape((2, 256, 256))),

time: 124 us -> 124 us (level)
  blocking collectives: 44.9 us -> 46.9 us
    all_to_all x3, blocking collectives: 44.9 us -> 46.9 us  [exchange(): return lax.all_to_all(blocks, axes, 0, 0, tiled=True)]
where the time goes in v3:
time: 124 us
  blocking collectives  46.9 us (38%)
  starting transfers between devices  42.6 us (34%)
  waiting for transfers between devices  20.1 us (16%)
  Pallas kernels  8.16 us (7%)
  local copies, waits for them, and re-layouts  4.39 us (4%)
  between operations  1.52 us (1%)
    all_to_all x3, blocking collectives, exchange(): return lax.all_to_all(blocks, axes, 0, 0, tiled=True)  46.9 us
    ppermute x4, starting transfers between devices, swap(): return lax.ppermute(value, axis, [(0, 1), (1, 0)])  22.5 us
    all_to_all x2, starting transfers between devices, exchange(): return lax.all_to_all(blocks, axes, 0, 0, tiled=True)  20.1 us
    all_to_all x2, waiting for transfers between devices, exchange(): return lax.all_to_all(blocks, axes, 0, 0, tiled=True)  12 us
    pallas_call x10, Pallas kernels, call(): pl.pallas_call(kernel, out_shape=outs, in_specs=ins, compiler_params=pltp...  8.16 us
    ppermute x4, waiting for transfers between devices, swap(): return lax.ppermute(value, axis, [(0, 1), (1, 0)])  8.11 us
    unnamed x24, local copies, waits for them, and re-layouts  4.22 us
  transfers between devices with their start and end apart: 6, of which 5 were waited for; matrix products, arithmetic and copies ran while one was open for 0% of the time, Pallas kernels for 3%

profile of v3, /device:TPU:1, one launch (start us, length us, event | category | flops | bytes accessed | tf_op | source)
XLA Modules:
  0.0 123.9 jit_solution(13680764641516144848)
XLA Ops:
  0.6 1.4 %mask.1 = bf16[32,8,256]{2,1,0:T(8,128)(2,1)} custom-call(bf16[8,256]{1,0:T(8,128)(2,1)} %bitcast.30, bf16[8,256]{1,0:T(8,128)(2,1)} %bitcast.32), custom_call_target="tpu_custom_call" | custom-call | flops 10000 | bytes 140000 | tf_op jit(solution)/shard_map/mask/pallas_call | solution.py:180
  2.0 16.1 %all-to-all-start = ((bf16[32,8,256]{2,1,0:T(8,128)(2,1)}), bf16[32,8,256]{2,1,0:T(8,128)(2,1)S(1)}, u32[]{:S(2)}, u32[]{:S(2)}) async-start(bf16[32,8,256]{2,1,0:T(8,128)(2,1)} %mask.1), calls=%async_computation | async-start | bytes 262144 | tf_op jit(solution)/shard_map/all_to_all | solution.py:20
  18.8 1.0 copy-done
  19.8 0.9 copy-done.3
  20.7 0.9 copy-done.4
  21.6 0.7 copy-done.10
  22.3 0.7 copy-done.11
  23.0 1.2 layout.1
  24.2 5.7 %all-to-all-done.delta_ref = bf16[32,8,256]{2,1,0:T(8,128)(2,1)S(1)} async-done(((bf16[32,8,256]{2,1,0:T(8,128)(2,1)}), bf16[32,8,256]{2,1,0:T(8,128)(2,1)S(1)}, u32[]{:S(2)}, u32[]{:S(2)}) %all-to-all-start) | async-done | bytes 131104 | tf_op jit(solution)/shard_map/all_to_all | solution.py:20
  29.9 0.9 send.1
  30.8 5.4 %collective-permute-start = (bf16[2048,128]{1,0:T(8,128)(2,1)S(1)}, bf16[2048,128]{1,0:T(8,128)(2,1)S(1)}, u32[]{:S(2)}, u32[]{:S(2)}) collective-permute-start(bf16[2048,128]{1,0:T(8,128)(2,1)S(1)} %send.1), channel_id=1, source_target_pairs={{0,1},{1,0},{2,3},{3,2},{4,5},{5,4},{6,7},{7,6},{8,9},{9,8},{10,11... | collective-permute-start | bytes 1572872 | tf_op jit(solution)/shard_map/ppermute | solution.py:28
  36.2 0.9 keep.1.keep_ref
  37.1 0.0 copy-start.1
  37.2 0.5 collective-permute-done.recv_ref
  37.7 0.9 pair.1
  38.7 4.0 %all-to-all-start.1 = ((bf16[4,2,256,128]{3,2,1,0:T(8,128)(2,1)}), bf16[4,2,256,128]{3,2,1,0:T(8,128)(2,1)S(1)}, u32[]{:S(2)}, u32[]{:S(2)}) async-start(bf16[4,2,256,128]{3,2,1,0:T(8,128)(2,1)} %bitcast.5), calls=%async_computation.1 | async-start | bytes 1048576 | tf_op jit(solution)/shard_map/all_to_all | solution.py:20
  42.8 2.6 %collective-permute-start.2 = (bf16[144,1792]{1,0:T(8,128)(2,1)S(1)}, bf16[144,1792]{1,0:T(8,128)(2,1)S(1)}, u32[]{:S(2)}, u32[]{:S(2)}) collective-permute-start(bf16[144,1792]{1,0:T(8,128)(2,1)S(1)} %bundle.1.own_ref), channel_id=1, source_target_pairs={{0,1},{1,0},{2,3},{3,2},{4,5},{5,4},{6,7},{7,6},{8,9},{9,8},{10,11... | collective-permute-start | bytes 1548296 | tf_op jit(solution)/shard_map/ppermute | solution.py:28
  45.3 6.2 %all-to-all-done.1 = bf16[4,2,256,128]{3,2,1,0:T(8,128)(2,1)S(1)} async-done(((bf16[4,2,256,128]{3,2,1,0:T(8,128)(2,1)}), bf16[4,2,256,128]{3,2,1,0:T(8,128)(2,1)S(1)}, u32[]{:S(2)}, u32[]{:S(2)}) %all-to-all-start.1) | async-done | bytes 524320 | tf_op jit(solution)/shard_map/all_to_all | solution.py:20
  51.6 0.1 convert_reduce_fusion
  51.7 7.9 %collective-permute-start.1 = (bf16[256,128]{1,0:T(8,128)(2,1)S(1)}, bf16[256,128]{1,0:T(8,128)(2,1)S(1)}, u32[]{:S(2)}, u32[]{:S(2)}) collective-permute-start(bf16[256,128]{1,0:T(8,128)(2,1)S(1)} %fusion), channel_id=1, source_target_pairs={{0,2},{2,0},{1,3},{3,1},{4,6},{6,4},{5,7},{7,5},{8,10},{10,8},{9,1... | collective-permute-start | bytes 196616 | tf_op jit(solution)/shard_map/ppermute | solution.py:28
  59.7 0.4 turn.1
  60.0 7.1 %collective-permute-done.1.recv_ref = bf16[256,128]{1,0:T(8,128)(2,1)S(1)} collective-permute-done((bf16[256,128]{1,0:T(8,128)(2,1)S(1)}, bf16[256,128]{1,0:T(8,128)(2,1)S(1)}, u32[]{:S(2)}, u32[]{:S(2)}) %collective-permute-start.1) | collective-permute-done | bytes 65568 | tf_op jit(solution)/shard_map/ppermute | solution.py:28
  67.2 0.4 terms.1
  67.5 14.2 %all_to_all.25 = bf16[32,64,128]{2,1,0:T(8,128)(2,1)S(1)} all-to-all(bf16[32,64,128]{2,1,0:T(8,128)(2,1)S(1)} %bitcast.25), channel_id=1, replica_groups=mesh['y'=4,'zm'=2,'zna'=2,'znb'=2,'x'=4,'zh'=2,'core'=2] {'znb','y','x'}, dimensions={0} | all-to-all | bytes 1048576 | tf_op jit(solution)/shard_map/all_to_all | solution.py:20
  81.7 0.1 reduce_sum.34
  81.8 19.2 %all_to_all.26 = bf16[8,64,128]{2,1,0:T(8,128)(2,1)S(1)} all-to-all(bf16[8,64,128]{2,1,0:T(8,128)(2,1)S(1)} %broadcast_in_dim.4), channel_id=1, replica_groups=mesh['y'=4,'zm'=2,'zna'=2,'znb'=2,'x'=4,'zh'=2,'core'=2] {'zna','zm','zh'}, dimensions={0} | all-to-all | bytes 262144 | tf_op jit(solution)/shard_map/all_to_all | solution.py:20
  101.1 0.1 broadcast_in_dim.5
  101.2 13.5 %all_to_all.27 = bf16[32,64,128]{2,1,0:T(8,128)(2,1)S(1)} all-to-all(bf16[32,64,128]{2,1,0:T(8,128)(2,1)S(1)} %broadcast_in_dim.5), channel_id=1, replica_groups=mesh['y'=4,'zm'=2,'zna'=2,'znb'=2,'x'=4,'zh'=2,'core'=2] {'znb','y','x'}, dimensions={0} | all-to-all | bytes 1048576 | tf_op jit(solution)/shard_map/all_to_all | solution.py:20
  114.7 6.6 %collective-permute-start.3 = (bf16[2048,128]{1,0:T(8,128)(2,1)S(1)}, bf16[2048,128]{1,0:T(8,128)(2,1)S(1)}, u32[]{:S(2)}, u32[]{:S(2)}) collective-permute-start(bf16[2048,128]{1,0:T(8,128)(2,1)S(1)} %bitcast.23), channel_id=1, source_target_pairs={{0,1},{1,0},{2,3},{3,2},{4,5},{5,4},{6,7},{7,6},{8,9},{9,8},{10,11... | collective-permute-start | bytes 1572872 | tf_op jit(solution)/shard_map/ppermute | solution.py:28
  121.4 1.0 widen_own.1
  122.4 0.5 collective-permute-done.3.recv_ref
  122.9 1.0 widen_recv.1
  (24 shorter events, 0.2 us)
Async XLA Ops:
  2.0 27.9 %all-to-all-start = ((bf16[32,8,256]{2,1,0:T(8,128)(2,1)}), bf16[32,8,256]{2,1,0:T(8,128)(2,1)S(1)}, u32[]{:S(2)}, u32[]{:S(2)}) async-start(bf16[32,8,256]{2,1,0:T(8,128)(2,1)} %mask.1), calls=%async_computation | async-start | bytes 262144 | tf_op jit(solution)/shard_map/all_to_all | solution.py:20
  18.8 1.0 copy-start
  19.8 0.9 copy-start.3
  20.7 0.9 copy-start.4
  21.6 0.7 copy-start.10
  22.3 0.7 copy-start.11
  30.8 6.9 %collective-permute-start = (bf16[2048,128]{1,0:T(8,128)(2,1)S(1)}, bf16[2048,128]{1,0:T(8,128)(2,1)S(1)}, u32[]{:S(2)}, u32[]{:S(2)}) collective-permute-start(bf16[2048,128]{1,0:T(8,128)(2,1)S(1)} %send.1), channel_id=1, source_target_pairs={{0,1},{1,0},{2,3},{3,2},{4,5},{5,4},{6,7},{7,6},{8,9},{9,8},{10,11... | collective-permute-start | bytes 1572872 | tf_op jit(solution)/shard_map/ppermute | solution.py:28
  37.1 5.6 %copy-start.1 = (bf16[1,128,768]{2,1,0:T(8,128)(2,1)S(1)}, bf16[1,128,768]{2,1,0:T(8,128)(2,1)}, u32[]{:S(2)}) copy-start(bf16[1,128,768]{2,1,0:T(8,128)(2,1)} %param.24) | copy-start | bytes 589828
  37.1 5.5 %copy-start.2 = (bf16[1,128,768]{2,1,0:T(8,128)(2,1)S(1)}, bf16[1,128,768]{2,1,0:T(8,128)(2,1)}, u32[]{:S(2)}) copy-start(bf16[1,128,768]{2,1,0:T(8,128)(2,1)} %param.25) | copy-start | bytes 589828
  37.1 5.5 %copy-start.5 = (bf16[1,128,256]{2,1,0:T(8,128)(2,1)S(1)}, bf16[1,128,256]{2,1,0:T(8,128)(2,1)}, u32[]{:S(2)}) copy-start(bf16[1,128,256]{2,1,0:T(8,128)(2,1)} %param.23) | copy-start | bytes 196612
  37.1 5.5 %copy-start.6 = (bf16[1,8,256]{2,1,0:T(8,128)(2,1)S(1)}, bf16[1,8,256]{2,1,0:T(8,128)(2,1)}, u32[]{:S(2)}) copy-start(bf16[1,8,256]{2,1,0:T(8,128)(2,1)} %param.13) | copy-start | bytes 12292
  37.2 5.5 %copy-start.7 = (bf16[1,8,256]{2,1,0:T(8,128)(2,1)S(1)}, bf16[1,8,256]{2,1,0:T(8,128)(2,1)}, u32[]{:S(2)}) copy-start(bf16[1,8,256]{2,1,0:T(8,128)(2,1)} %param.14) | copy-start | bytes 12292
  37.2 5.5 %copy-start.8 = (bf16[1,8,256]{2,1,0:T(8,128)(2,1)S(1)}, bf16[1,8,256]{2,1,0:T(8,128)(2,1)}, u32[]{:S(2)}) copy-start(bf16[1,8,256]{2,1,0:T(8,128)(2,1)} %param.15) | copy-start | bytes 12292
  37.2 5.5 %copy-start.9 = (bf16[1,8,256]{2,1,0:T(8,128)(2,1)S(1)}, bf16[1,8,256]{2,1,0:T(8,128)(2,1)}, u32[]{:S(2)}) copy-start(bf16[1,8,256]{2,1,0:T(8,128)(2,1)} %param.16) | copy-start | bytes 12292
  38.7 12.9 %all-to-all-start.1 = ((bf16[4,2,256,128]{3,2,1,0:T(8,128)(2,1)}), bf16[4,2,256,128]{3,2,1,0:T(8,128)(2,1)S(1)}, u32[]{:S(2)}, u32[]{:S(2)}) async-start(bf16[4,2,256,128]{3,2,1,0:T(8,128)(2,1)} %bitcast.5), calls=%async_computation.1 | async-start | bytes 1048576 | tf_op jit(solution)/shard_map/all_to_all | solution.py:20
  42.8 16.9 %collective-permute-start.2 = (bf16[144,1792]{1,0:T(8,128)(2,1)S(1)}, bf16[144,1792]{1,0:T(8,128)(2,1)S(1)}, u32[]{:S(2)}, u32[]{:S(2)}) collective-permute-start(bf16[144,1792]{1,0:T(8,128)(2,1)S(1)} %bundle.1.own_ref), channel_id=1, source_target_pairs={{0,1},{1,0},{2,3},{3,2},{4,5},{5,4},{6,7},{7,6},{8,9},{9,8},{10,11... | collective-permute-start | bytes 1548296 | tf_op jit(solution)/shard_map/ppermute | solution.py:28
  51.7 15.5 %collective-permute-start.1 = (bf16[256,128]{1,0:T(8,128)(2,1)S(1)}, bf16[256,128]{1,0:T(8,128)(2,1)S(1)}, u32[]{:S(2)}, u32[]{:S(2)}) collective-permute-start(bf16[256,128]{1,0:T(8,128)(2,1)S(1)} %fusion), channel_id=1, source_target_pairs={{0,2},{2,0},{1,3},{3,1},{4,6},{6,4},{5,7},{7,5},{8,10},{10,8},{9,1... | collective-permute-start | bytes 196616 | tf_op jit(solution)/shard_map/ppermute | solution.py:28
  114.7 8.2 %collective-permute-start.3 = (bf16[2048,128]{1,0:T(8,128)(2,1)S(1)}, bf16[2048,128]{1,0:T(8,128)(2,1)S(1)}, u32[]{:S(2)}, u32[]{:S(2)}) collective-permute-start(bf16[2048,128]{1,0:T(8,128)(2,1)S(1)} %bitcast.23), channel_id=1, source_target_pairs={{0,1},{1,0},{2,3},{3,2},{4,5},{5,4},{6,7},{7,6},{8,9},{9,8},{10,11... | collective-permute-start | bytes 1572872 | tf_op jit(solution)/shard_map/ppermute | solution.py:28
